TPU v7x, 512 devices: a whole 4x4x16 slice. The times are simulated.
512 devices in a mesh: inp: 4 (over y), out: 8 (over z_hi, core), dep: 16 (over z_lo, x).
Axes of the slice: x: 4, y: 4, z: 16 (z_hi: 4, z_lo: 4; z = z_hi * 4 + z_lo), core: 2. Of those that a mesh axis runs over, the one named last changes fastest.
Arguments:
- x_saved: bfloat16 [1024, 8192], P('dep', ('inp', 'out')), may hold values from -6 to 6
- gate_pre: bfloat16 [1024, 14336], P(('inp', 'out'), 'dep'), may hold values from -6 to 6
- up_pre: bfloat16 [1024, 14336], P(('inp', 'out'), 'dep'), may hold values from -6 to 6
- out_grad: bfloat16 [1024, 8192], P('dep', ('inp', 'out')), may hold values from -6 to 6
- gate_weight: bfloat16 [8192, 14336], P(('inp', 'out'), 'dep'), may hold values from -0.09375 to 0.09375
- up_weight: bfloat16 [8192, 14336], P(('inp', 'out'), 'dep'), may hold values from -0.09375 to 0.09375
- down_weight: bfloat16 [14336, 8192], P('dep', ('inp', 'out')), may hold values from -0.0625 to 0.0625
- gate_mask: int32 [64, 112], P(('inp', 'out'), 'dep'), may hold values 0 or 1
- up_mask: int32 [64, 112], P(('inp', 'out'), 'dep'), may hold values 0 or 1
- down_mask: int32 [112, 64], P('dep', ('inp', 'out')), may hold values 0 or 1
Outputs:
- input_grad: bfloat16 [1024, 8192], P('dep', ('inp', 'out'))
- gate_weight_grad: float32 [8192, 14336], P(('inp', 'out'), 'dep')
- up_weight_grad: float32 [8192, 14336], P(('inp', 'out'), 'dep')
- down_weight_grad: float32 [14336, 8192], P('dep', ('inp', 'out'))
Inputs may be any that keep to these rules, and one draw needn't show every extreme that they name: `gate_mask`: 1 keeps a 128 x 128 tile of the gate projection, 0 drops it. `up_mask`: 1 keeps a 128 x 128 tile of the up projection, 0 drops it. `down_mask`: 1 keeps a 128 x 128 tile of the down projection, 0 drops it.
All inputs are finite; a program needn't handle non-finite values. No bound on the sum of `gate_mask` or of `up_mask` or of `down_mask` on one device may be relied on, other than what follows from the above.
Results may differ from a plain program's by a relative error of at most 0.0049.
Values may be sent and summed in bfloat16 or wider, within the bound.
A program may use at most 64 MiB of HBM per device.

v0:
```python
import jax
import jax.numpy as jnp
from jax import lax
from jax.sharding import PartitionSpec as P

TILE = 128


def expand(tiles):
    return jnp.repeat(jnp.repeat(tiles, TILE, 0), TILE, 1).astype(jnp.bfloat16)


def contract_rows(left, right):
    return lax.dot_general(
        left, right, (((0,), (0,)), ((), ())), preferred_element_type=jnp.float32
    )


def contract_cols(left, right):
    return lax.dot_general(
        left, right, (((1,), (1,)), ((), ())), preferred_element_type=jnp.float32
    )


def hidden_terms(hidden_grad, gate_pre, up_pre):
    gate_val = gate_pre.astype(jnp.float32)
    up_val = up_pre.astype(jnp.float32)
    sigma = jax.nn.sigmoid(gate_val)
    gate_grad = (hidden_grad * up_val * sigma * (1.0 + gate_val * (1.0 - sigma))).astype(
        jnp.bfloat16
    )
    up_grad = (hidden_grad * gate_val * sigma).astype(jnp.bfloat16)
    hidden_act = (gate_val * sigma * up_val).astype(jnp.bfloat16)
    return (gate_grad, up_grad, hidden_act)


def on_device(
    x_saved,
    gate_pre,
    up_pre,
    out_grad,
    gate_weight,
    up_weight,
    down_weight,
    gate_mask,
    up_mask,
    down_mask,
):
    gate_keep = expand(gate_mask)
    up_keep = expand(up_mask)
    down_keep = expand(down_mask)
    gate_eff = gate_weight * gate_keep
    up_eff = up_weight * up_keep
    down_eff = down_weight * down_keep
    cotangent = lax.all_gather(out_grad, "dep", axis=0, tiled=True)
    partial_hidden = contract_cols(cotangent, down_eff)
    hidden_grad = lax.psum_scatter(partial_hidden, ("inp", "out"), scatter_dimension=0, tiled=True)
    gate_grad, up_grad, hidden_act = hidden_terms(hidden_grad, gate_pre, up_pre)
    gate_rows, up_rows, act_rows = (
        lax.all_gather(gate_grad, ("inp", "out"), axis=0, tiled=True),
        lax.all_gather(up_grad, ("inp", "out"), axis=0, tiled=True),
        lax.all_gather(hidden_act, ("inp", "out"), axis=0, tiled=True),
    )
    gate_part = gate_rows
    up_part = up_rows
    input_grad = lax.psum_scatter(
        contract_cols(gate_part, gate_eff) + contract_cols(up_part, up_eff),
        "dep",
        scatter_dimension=0,
        tiled=True,
    ).astype(jnp.bfloat16)
    down_weight_grad = contract_rows(act_rows, cotangent) * down_keep.astype(jnp.float32)
    piece = lax.all_gather(x_saved, "dep", axis=0, tiled=True)
    gate_part = gate_rows
    up_part = up_rows
    gate_sum = contract_rows(piece, gate_part)
    up_sum = contract_rows(piece, up_part)
    gate_weight_grad = gate_sum * gate_keep.astype(jnp.float32)
    up_weight_grad = up_sum * up_keep.astype(jnp.float32)
    return (input_grad, gate_weight_grad, up_weight_grad, down_weight_grad)


def solution(mesh):
    return jax.shard_map(
        on_device,
        mesh=mesh,
        in_specs=(
            P("dep", ("inp", "out")),
            P(("inp", "out"), "dep"),
            P(("inp", "out"), "dep"),
            P("dep", ("inp", "out")),
            P(("inp", "out"), "dep"),
            P(("inp", "out"), "dep"),
            P("dep", ("inp", "out")),
            P(("inp", "out"), "dep"),
            P(("inp", "out"), "dep"),
            P("dep", ("inp", "out")),
        ),
        out_specs=(
            P("dep", ("inp", "out")),
            P(("inp", "out"), "dep"),
            P(("inp", "out"), "dep"),
            P("dep", ("inp", "out")),
        ),
        check_vma=False,
    )
```

profile of v0, /device:TPU:24, one launch (start us, length us, event | category | flops | bytes accessed | tf_op | source)
XLA Modules:
  0.0 517.7 jit_solution(16612209569078845278)
XLA Ops:
  7.2 0.0 reduce-scatter.7.cloned.1.call-start
  7.2 0.7 convert_element_type.60
  7.9 0.1 copy.35
  8.0 46.7 %all_gather.15 = bf16[1024,256]{1,0:T(8,128)(2,1)S(1)} all-gather(bf16[64,256]{1,0:T(8,128)(2,1)} %param.13), channel_id=1, replica_groups=mesh['inp'=4,'out'=8,'dep'=16] {'dep'}, dimensions={0}, use_global_device_ids=true | all-gather | bytes 557056 | tf_op jit(solution)/shard_map/all_gather | solution.py:55
  54.7 1.1 broadcast_in_dim.19
  55.9 3.5 convolution_bitcast_fusion
  59.4 5.0 copy.44
  64.4 0.0 copy-start.4
  64.4 0.0 copy-start.5
  64.4 0.0 copy-start.7
  64.4 0.0 copy-start.2
  64.4 0.0 copy-start.8
  64.4 0.0 copy-start.3
  64.4 0.0 reduce-scatter.7.cloned.1.call-update
  64.5 0.0 all-gather.4.cloned.1.call-start
  64.5 131.3 %reduce-scatter.7.cloned.1.call-done = f32[32,896]{1,0:T(8,128)} async-done(((f32[1024,896]{1,0:T(8,128)}), f32[32,896]{1,0:T(8,128)}) %reduce-scatter.7.cloned.1.call-update) | async-done | bytes 114704 | tf_op jit(solution)/shard_map/reduce_scatter | solution.py:57
  195.8 0.0 copy-done.4
  195.8 0.0 copy-done.5
  195.9 1.6 fusion.12
  197.5 0.0 all-gather.4.cloned.1.call-update
  197.5 0.0 all-gather.6.cloned.1.call-start
  197.5 0.7 all-gather.6.cloned.1.call-update
  198.2 0.0 all-gather.8.cloned.1.call-start
  198.3 0.5 all-gather.8.cloned.1.call-update
  198.8 0.0 reduce-scatter.5.cloned.1.call-start
  198.9 0.0 copy-done.7
  198.9 0.1 copy.37
  199.0 0.1 broadcast_bitcast_fusion.1
  199.1 0.0 copy-done.2
  199.1 0.2 copy.38
  199.3 0.0 copy-done.8
  199.3 0.1 copy.40
  199.4 0.1 broadcast_bitcast_fusion
  199.5 0.0 copy-done.3
  199.5 0.2 copy.41
  199.8 71.8 %all-gather.4.cloned.1.call-done = bf16[1024,896]{1,0:T(8,128)(2,1)} async-done(((bf16[32,896]{1,0:T(8,128)(2,1)}), bf16[1024,896]{1,0:T(8,128)(2,1)}) %all-gather.4.cloned.1.call-update) | async-done | bytes 1835024 | tf_op jit(solution)/shard_map/all_gather | solution.py:60
  271.7 2.2 fusion.13
  273.9 0.0 copy-start.6
  273.9 72.8 %all-gather.6.cloned.1.call-done = bf16[1024,896]{1,0:T(8,128)(2,1)} async-done(((bf16[32,896]{1,0:T(8,128)(2,1)}), bf16[1024,896]{1,0:T(8,128)(2,1)}) %all-gather.6.cloned.1.call-update) | async-done | bytes 1835024 | tf_op jit(solution)/shard_map/all_gather | solution.py:61
  346.7 3.2 convolution_add_fusion
  349.9 0.0 copy-start
  349.9 0.0 reduce-scatter.5.cloned.1.call-update
  350.0 0.0 copy-done.6
  350.0 44.4 %all_gather.18 = bf16[1024,256]{1,0:T(8,128)(2,1)S(1)} all-gather(bf16[64,256]{1,0:T(8,128)(2,1)S(1)} %copy-done.6), channel_id=1, replica_groups=mesh['inp'=4,'out'=8,'dep'=16] {'dep'}, dimensions={0}, use_global_device_ids=true | all-gather | bytes 557056 | tf_op jit(solution)/shard_map/all_gather | solution.py:73
  394.4 0.0 copy-done
  394.4 1.6 fusion
  396.0 0.0 copy-start.1
  396.0 2.5 copy.42
  398.6 0.0 copy-done.1
  398.6 1.6 fusion.1
  400.2 2.4 copy.43
  402.6 18.5 %all-gather.8.cloned.1.call-done = bf16[1024,896]{1,0:T(8,128)(2,1)} async-done(((bf16[32,896]{1,0:T(8,128)(2,1)}), bf16[1024,896]{1,0:T(8,128)(2,1)}) %all-gather.8.cloned.1.call-update) | async-done | bytes 1835024 | tf_op jit(solution)/shard_map/all_gather | solution.py:62
  421.1 3.1 convolution_multiply_fusion
  424.2 85.5 %reduce-scatter.5.cloned.1.call-done = f32[64,256]{1,0:T(8,128)} async-done(((f32[1024,256]{1,0:T(8,128)}), f32[64,256]{1,0:T(8,128)}) %reduce-scatter.5.cloned.1.call-update) | async-done | bytes 65552 | tf_op jit(solution)/shard_map/reduce_scatter | solution.py:66
  509.7 1.5 convert_element_type.73
  (9 shorter events, 0.2 us)
Async XLA Ops:
  7.2 188.7 %reduce-scatter.7.cloned.1.call-start = ((), (), s32[]{:S(2)}) async-start(), calls=%async_computation.6 | async-start | bytes 3784704 | tf_op jit(solution)/shard_map/reduce_scatter | solution.py:57
  64.4 131.4 %copy-start.4 = (bf16[32,896]{1,0:T(8,128)(2,1)S(1)}, bf16[32,896]{1,0:T(8,128)(2,1)}, u32[]{:S(2)}) copy-start(bf16[32,896]{1,0:T(8,128)(2,1)} %param.11) | copy-start | bytes 172036
  64.4 131.4 %copy-start.5 = (bf16[32,896]{1,0:T(8,128)(2,1)S(1)}, bf16[32,896]{1,0:T(8,128)(2,1)}, u32[]{:S(2)}) copy-start(bf16[32,896]{1,0:T(8,128)(2,1)} %param.12) | copy-start | bytes 172036
  64.4 134.4 %copy-start.7 = (s32[2,7]{1,0:T(2,128)S(1)}, s32[2,7]{1,0:T(2,128)}, u32[]{:S(2)}) copy-start(s32[2,7]{1,0:T(2,128)} %param.17) | copy-start | bytes 172
  64.4 134.7 %copy-start.2 = (bf16[256,896]{1,0:T(8,128)(2,1)S(1)}, bf16[256,896]{1,0:T(8,128)(2,1)}, u32[]{:S(2)}) copy-start(bf16[256,896]{1,0:T(8,128)(2,1)} %param.14) | copy-start | bytes 1376260
  64.4 134.9 %copy-start.8 = (s32[2,7]{1,0:T(2,128)S(1)}, s32[2,7]{1,0:T(2,128)}, u32[]{:S(2)}) copy-start(s32[2,7]{1,0:T(2,128)} %param.18) | copy-start | bytes 172
  64.4 135.1 %copy-start.3 = (bf16[256,896]{1,0:T(8,128)(2,1)S(1)}, bf16[256,896]{1,0:T(8,128)(2,1)}, u32[]{:S(2)}) copy-start(bf16[256,896]{1,0:T(8,128)(2,1)} %param.15) | copy-start | bytes 1376260
  64.5 207.2 %all-gather.4.cloned.1.call-start = ((), (), s32[]{:S(2)}) async-start(), calls=%async_computation.2 | async-start | bytes 1892352 | tf_op jit(solution)/shard_map/all_gather | solution.py:60
  197.5 149.2 %all-gather.6.cloned.1.call-start = ((), (), s32[]{:S(2)}) async-start(), calls=%async_computation.3 | async-start | bytes 1892352 | tf_op jit(solution)/shard_map/all_gather | solution.py:61
  198.2 222.9 %all-gather.8.cloned.1.call-start = ((), (), s32[]{:S(2)}) async-start(), calls=%async_computation.5 | async-start | bytes 1892352 | tf_op jit(solution)/shard_map/all_gather | solution.py:62
  198.8 310.9 %reduce-scatter.5.cloned.1.call-start = ((), (), s32[]{:S(2)}) async-start(), calls=%async_computation.4 | async-start | bytes 1114112 | tf_op jit(solution)/shard_map/reduce_scatter | solution.py:66
  273.9 76.1 %copy-start.6 = (bf16[64,256]{1,0:T(8,128)(2,1)S(1)}, bf16[64,256]{1,0:T(8,128)(2,1)}, u32[]{:S(2)}) copy-start(bf16[64,256]{1,0:T(8,128)(2,1)} %param.10) | copy-start | bytes 98308
  349.9 44.5 %copy-start = (bf16[1024,896]{1,0:T(8,128)(2,1)S(1)}, bf16[1024,896]{1,0:T(8,128)(2,1)}, u32[]{:S(2)}) copy-start(bf16[1024,896]{1,0:T(8,128)(2,1)} %all-gather.4.cloned.1.call-done) | copy-start | bytes 5505028
  396.0 2.6 copy-start.1
Sparse Core Ops, SparseCore 0:
  64.6 131.2 reduce-scatter.6
  200.0 71.6 all-gather.3
  275.8 70.8 all-gather.5
  350.2 70.8 all-gather.7
  424.0 85.6 reduce-scatter.4
where the time goes:
time: 518 us
  waiting for transfers between devices  381 us (74%)
  blocking collectives  91.1 us (18%)
  matrix products  15.3 us (3%)
  between operations  13.9 us (3%)
  local copies, waits for them, and re-layouts  12.1 us (2%)
    reduce_scatter x1, waiting for transfers between devices, on_device(): lax.psum_scatter(partial_hidden, ('inp', 'out'), scatter_dimension=0, til...  131 us
    reduce_scatter x1, waiting for transfers between devices, on_device(): lax.psum_scatter(contract_cols(gate_part, gate_eff) + contract_cols(up_pa...  85.5 us
    all_gather x1, waiting for transfers between devices, on_device(): lax.all_gather(up_grad, ('inp', 'out'), axis=0, tiled=True)  72.8 us
    all_gather x1, waiting for transfers between devices, on_device(): lax.all_gather(gate_grad, ('inp', 'out'), axis=0, tiled=True)  71.8 us
    all_gather x1, blocking collectives, on_device(): cotangent = lax.all_gather(out_grad, 'dep', axis=0, tiled=True)  46.7 us
    all_gather x1, blocking collectives, on_device(): piece = lax.all_gather(x_saved, 'dep', axis=0, tiled=True)  44.4 us
    all_gather x1, waiting for transfers between devices, on_device(): lax.all_gather(hidden_act, ('inp', 'out'), axis=0, tiled=True)  18.5 us
    unnamed x27, local copies, waits for them, and re-layouts  10.6 us
  transfers between devices with their start and end apart: 5, of which 5 were waited for; matrix products, arithmetic and copies ran while one was open for 3% of the time, Pallas kernels for 0%

commit v1 on v0

v1 whole, which is shorter than its diff:
```python
import functools

import jax
import jax.numpy as jnp
from jax import lax
from jax.experimental import pallas as pl
from jax.experimental.pallas import tpu as pltpu
from jax.sharding import PartitionSpec as P

TILE = 128
MESH = pl.DeviceIdType.MESH
F32 = jnp.float32
BF16 = jnp.bfloat16
NT = (((1,), (1,)), ((), ()))
TN = (((0,), (0,)), ((), ()))


def dot(left, right, dims):
    return lax.dot_general(left, right, dims, preferred_element_type=F32)


class Sems:
    def __init__(self, send, recv):
        self.send, self.recv = send, recv
        self.sends = self.recvs = 0
        self.started = []

    def take(self, count=1):
        first = self.recvs
        self.recvs += count
        return first

    def start(self, src, dst, slot, device):
        copy = pltpu.make_async_remote_copy(
            src_ref=src,
            dst_ref=dst,
            send_sem=self.send.at[self.sends],
            recv_sem=self.recv.at[slot],
            device_id=device,
            device_id_type=MESH,
        )
        self.sends += 1
        copy.start()
        self.started.append(copy)

    def wait(self, dst, slot, device):
        pltpu.make_async_remote_copy(
            src_ref=dst,
            dst_ref=dst,
            send_sem=self.send.at[0],
            recv_sem=self.recv.at[slot],
            device_id=device,
            device_id_type=MESH,
        ).wait_recv()

    def drain(self):
        for copy in self.started:
            copy.wait_send()


def keep_tiles(ref, mask, where=()):
    rows, cols = mask.shape
    for i in range(rows):
        for j in range(cols):
            at = (*where, pl.ds(i * TILE, TILE), pl.ds(j * TILE, TILE))
            ref[at] = (ref[at].astype(F32) * mask[i, j].astype(F32)).astype(ref.dtype)


def kernel(
    x_in, g_in, u_in, og_in, gw_in, uw_in, dw_in, gm, um, dm,
    ig_out, gwg_out, uwg_out, dwg_out,
    cot, cot_other, xs, act, gu, g_val, u_val, gw, uw, dw, f_gate, f_up,
    part_own, part_send, part_recv, sum_send, sum_recv,
    ig_own, ig_send, ig_recv, ig_mine, zl_send, zl_recv, ig_res,
    gwg, uwg, dwg, local, send, recv, zl_ss, zl_rs,
):
    y = lax.axis_index("inp")
    out = lax.axis_index("out")
    dep = lax.axis_index("dep")
    zh, c = out // 2, out % 2
    zl, x = dep // 4, dep % 4
    other = 1 - c
    plus = lambda v, k: (v + k) % 4
    at_core = {"out": zh * 2 + other}
    at_y = lambda k: {"inp": plus(y, k)}
    at_zh = lambda k: {"out": plus(zh, k) * 2 + c}
    at_x = lambda k: {"dep": zl * 4 + plus(x, k)}
    at_zl = lambda k, core: {"out": zh * 2 + core, "dep": plus(zl, k) * 4 + x}

    loads = []

    def load(src, dst):
        copy = pltpu.make_async_copy(src, dst, local.at[len(loads)])
        copy.start()
        loads.append(copy)
        return copy

    ld_og = load(og_in.at[pl.ds(c, 1)], cot.at[c, zl, pl.ds(x, 1)])
    ld_g = load(g_in, g_val)
    ld_u = load(u_in, u_val)
    ld_dw = load(dw_in, dw.at[c])
    ld_x = load(x_in, xs.at[:, zl, x])
    ld_gw = load(gw_in, gw)
    ld_uw = load(uw_in, uw)

    peers = [at_core]
    for k in (1, 2, 3):
        peers += [at_y(k), at_zh(k), at_x(k), at_zl(k, 0), at_zl(k, 1)]
    barrier = pltpu.get_barrier_semaphore()
    for device in peers:
        pl.semaphore_signal(barrier, inc=1, device_id=device, device_id_type=MESH)
    pl.semaphore_wait(barrier, len(peers))

    sems = Sems(send, recv)

    og_slot = sems.take(8)
    sems.start(og_in.at[other], cot.at[c, zl, x], og_slot + c, at_core)
    for k in (2, 1, 3):
        for h in (0, 1):
            sems.start(og_in.at[h], cot.at[c, zl, x], og_slot + 2 * k + c, at_zl(k, h))

    ld_g.wait()
    ld_u.wait()
    g = g_val[...].astype(F32)
    u = u_val[...].astype(F32)
    s = 1.0 / (1.0 + jnp.exp(-g))
    gs = g * s
    act[c, y, zh] = (gs * u).astype(BF16)
    f_up[...] = gs
    f_gate[...] = u * s * (1.0 + g * (1.0 - s))

    act_z = sems.take(4)
    act_y = sems.take(16)
    for k in (2, 1, 3):
        sems.start(act.at[c, y, zh], act.at[c, y, zh], act_z + k, at_zh(k))

    def act_to_y(kz):
        block = act.at[c, y, plus(zh, -kz)]
        for k in (2, 1, 3):
            sems.start(block, block, act_y + 4 * k + kz, at_y(k))

    act_to_y(0)

    ld_dw.wait()
    keep_tiles(dw, dm, (c,))
    dw_slot = sems.take()
    sems.start(dw.at[c], dw.at[c], dw_slot, at_core)

    ld_og.wait()
    sems.wait(cot.at[other, zl, x], og_slot + other, at_core)
    for k in (1, 3, 2):
        for f in (0, 1):
            sems.wait(cot.at[f, plus(zl, -k), x], og_slot + 2 * k + f, at_core)
    og_x = sems.take(4)
    for k in (2, 1, 3):
        sems.start(cot.at[:, :, x], cot.at[:, :, x], og_x + k, at_x(k))

    x_zl = sems.take(4)
    for k in (2, 1, 3):
        sems.start(x_in, xs.at[:, zl, x], x_zl + k, at_zl(k, c))

    ld_gw.wait()
    keep_tiles(gw, gm)
    ld_uw.wait()
    keep_tiles(uw, um)
    sems.wait(dw.at[other], dw_slot, at_core)
    for k in (1, 3):
        sems.wait(act.at[c, y, plus(zh, -k)], act_z + k, at_core)
        act_to_y(k)

    for k in (1, 3, 2):
        sems.wait(cot.at[:, :, plus(x, -k)], og_x + k, at_core)

    def partial(group):
        rows = [cot[f, group].reshape(128, 256) for f in (0, 1)]
        return dot(rows[0], dw[0], NT) + dot(rows[1], dw[1], NT)

    for k in (2, 1, 3):
        part_send[k - 1] = partial(plus(y, k)).astype(BF16).reshape(4, 32, 896)
    part_y = sems.take(16)
    for kz in (2, 1, 3, 0):
        block = plus(zh, kz)
        for k in (2, 1, 3):
            sems.start(
                part_send.at[k - 1, block], part_recv.at[k - 1, kz], part_y + 4 * k + kz, at_y(k)
            )
    part_own[...] = partial(y).reshape(4, 32, 896)

    cot_slot = sems.take()
    sems.start(cot.at[other], cot_other, cot_slot, at_core)

    ld_x.wait()
    for k in (1, 3, 2):
        sems.wait(xs.at[:, plus(zl, -k), x], x_zl + k, at_core)
    x_x = sems.take(4)
    for k in (2, 1, 3):
        sems.start(xs.at[:, :, x], xs.at[:, :, x], x_x + k, at_x(k))

    sems.wait(act.at[c, y, plus(zh, -2)], act_z + 2, at_core)
    act_to_y(2)

    sum_z = sems.take(4)
    total = None
    for kz in (2, 1, 3, 0):
        for k in (1, 3, 2):
            sems.wait(part_recv.at[k - 1, kz], part_y + 4 * k + kz, at_core)
        total = part_own[plus(zh, kz)]
        for k in (1, 2, 3):
            total = total + part_recv[k - 1, kz].astype(F32)
        if kz:
            sum_send[kz - 1] = total.astype(BF16)
            sems.start(sum_send.at[kz - 1], sum_recv.at[kz - 1], sum_z + kz, at_zh(kz))
    for kz in (1, 3, 2):
        sems.wait(sum_recv.at[kz - 1], sum_z + kz, at_core)
        total = total + sum_recv[kz - 1].astype(F32)

    gu[0, c, y, zh] = (total * f_gate[...]).astype(BF16)
    gu[1, c, y, zh] = (total * f_up[...]).astype(BF16)
    gu_z = sems.take(4)
    gu_y = sems.take(16)
    gu_c = sems.take(4)
    for k in (2, 1, 3):
        block = gu.at[:, c, y, zh]
        sems.start(block, block, gu_z + k, at_zh(k))

    def gu_to_y(kz):
        block = gu.at[:, c, y, plus(zh, -kz)]
        for k in (2, 1, 3):
            sems.start(block, block, gu_y + 4 * k + kz, at_y(k))

    gu_to_y(0)

    for k in (1, 3, 2):
        for kz in range(4):
            sems.wait(act.at[c, plus(y, -k), plus(zh, -kz)], act_y + 4 * k + kz, at_core)
    act_c = sems.take()
    sems.start(act.at[c], act.at[c], act_c, at_core)
    sems.wait(cot_other, cot_slot, at_core)
    sems.wait(act.at[other], act_c, at_core)
    mine = cot[c].reshape(512, 256)
    theirs = cot_other[...].reshape(512, 256)
    for i in range(7):
        at = pl.ds(i * TILE, TILE)
        tile = dot(act[c, :, :, :, at].reshape(512, TILE), mine, TN)
        tile = tile + dot(act[other, :, :, :, at].reshape(512, TILE), theirs, TN)
        for j in range(2):
            dwg[at, pl.ds(j * TILE, TILE)] = (
                tile[:, j * TILE : (j + 1) * TILE] * dm[i, j].astype(F32)
            )
    stores = [load(dwg, dwg_out)]

    for k in (1, 3, 2):
        sems.wait(xs.at[:, :, plus(x, -k)], x_x + k, at_core)

    for k in (1, 3, 2):
        sems.wait(gu.at[:, c, y, plus(zh, -k)], gu_z + k, at_core)
        gu_to_y(k)

    ig_x = sems.take(16)
    order = (0, 1, 3, 2)

    def reduce_x(k):
        group = plus(y, -k)
        for j in (1, 3, 2):
            sems.wait(ig_recv.at[k, j - 1], ig_x + 4 * k + j, at_core)
        value = ig_own[k]
        for j in (0, 1, 2):
            value = value + ig_recv[k, j].astype(F32)

        @pl.when(group == zl)
        def _():
            ig_mine[...] = value

        @pl.when(group != zl)
        def _():
            zl_send[k] = value.astype(BF16)
            to_zl(k).start()

    def to_zl(k):
        group = plus(y, -k)
        return pltpu.make_async_remote_copy(
            src_ref=zl_send.at[k],
            dst_ref=zl_recv.at[zl],
            send_sem=zl_ss.at[k],
            recv_sem=zl_rs.at[zl],
            device_id={"dep": group * 4 + x},
            device_id_type=MESH,
        )

    for n, k in enumerate(order):
        group = plus(y, -k)
        if k:
            for kz in (0, 1, 3, 2):
                sems.wait(gu.at[:, c, group, plus(zh, -kz)], gu_y + 4 * k + kz, at_core)
        sems.start(gu.at[:, c, group], gu.at[:, c, group], gu_c + k, at_core)
        sems.wait(gu.at[:, other, group], gu_c + k, at_core)
        gate = gu[0, :, group].reshape(256, 896)
        up = gu[1, :, group].reshape(256, 896)
        rows = (dot(gate, gw[...], NT) + dot(up, uw[...], NT)).reshape(2, 4, 32, 256)
        ig_send[k] = rows.astype(BF16)
        for j in (2, 1, 3):
            sems.start(
                ig_send.at[k, :, plus(x, j)], ig_recv.at[k, j - 1], ig_x + 4 * k + j, at_x(j)
            )
        ig_all = rows
        mine_rows = jnp.zeros((2, 32, 256), F32)
        for j in range(4):
            mine_rows = jnp.where(x == j, ig_all[:, j], mine_rows)
        ig_own[k] = mine_rows
        if n:
            reduce_x(order[n - 1])
        left = xs[:, group].reshape(256, 256)
        for total_ref, rows_in in ((gwg, gate), (uwg, up)):
            product = dot(left, rows_in, TN)
            if n:
                product = product + total_ref[...]
            total_ref[...] = product
    keep_tiles(gwg, gm)
    stores.append(load(gwg, gwg_out))
    keep_tiles(uwg, um)
    stores.append(load(uwg, uwg_out))
    reduce_x(order[-1])

    value = ig_mine[...]
    for k in (1, 2, 3):
        sems_at = plus(zl, k)
        pltpu.make_async_remote_copy(
            src_ref=zl_recv.at[sems_at],
            dst_ref=zl_recv.at[sems_at],
            send_sem=zl_ss.at[0],
            recv_sem=zl_rs.at[sems_at],
            device_id=at_core,
            device_id_type=MESH,
        ).wait_recv()
        value = value + zl_recv[sems_at].astype(F32)
    ig_res[...] = value.astype(BF16)
    stores.append(load(ig_res, ig_out))
    sems.drain()
    for k in range(4):

        @pl.when(plus(y, -k) != zl)
        def _():
            to_zl(k).wait_send()

    for copy in stores:
        copy.wait()


SENDS = 128
RECVS = 128


def on_device(x_saved, gate_pre, up_pre, out_grad, gate_weight, up_weight, down_weight, gate_mask, up_mask, down_mask):
    any_ = pl.BlockSpec(memory_space=pl.ANY)
    smem = pl.BlockSpec(memory_space=pltpu.SMEM)
    vmem = lambda *shape: pltpu.VMEM(shape, BF16)
    vmem32 = lambda *shape: pltpu.VMEM(shape, F32)
    outs = pl.pallas_call(
        kernel,
        name="backward",
        out_shape=(
            jax.ShapeDtypeStruct((2, 32, 256), BF16),
            jax.ShapeDtypeStruct((256, 896), F32),
            jax.ShapeDtypeStruct((256, 896), F32),
            jax.ShapeDtypeStruct((896, 256), F32),
        ),
        in_specs=[any_] * 7 + [smem] * 3,
        out_specs=(any_,) * 4,
        scratch_shapes=[
            vmem(2, 4, 4, 32, 256),
            vmem(4, 4, 32, 256),
            vmem(2, 4, 4, 32, 256),
            vmem(2, 4, 4, 32, 896),
            vmem(2, 2, 4, 4, 32, 896),
            vmem(32, 896),
            vmem(32, 896),
            vmem(256, 896),
            vmem(256, 896),
            vmem(2, 896, 256),
            vmem32(32, 896),
            vmem32(32, 896),
            vmem32(4, 32, 896),
            vmem(3, 4, 32, 896),
            vmem(3, 4, 32, 896),
            vmem(3, 32, 896),
            vmem(3, 32, 896),
            vmem32(4, 2, 32, 256),
            vmem(4, 2, 4, 32, 256),
            vmem(4, 3, 2, 32, 256),
            vmem32(2, 32, 256),
            vmem(4, 2, 32, 256),
            vmem(4, 2, 32, 256),
            vmem(2, 32, 256),
            vmem32(256, 896),
            vmem32(256, 896),
            vmem32(896, 256),
            pltpu.SemaphoreType.DMA((16,)),
            pltpu.SemaphoreType.DMA((SENDS,)),
            pltpu.SemaphoreType.DMA((RECVS,)),
            pltpu.SemaphoreType.DMA((4,)),
            pltpu.SemaphoreType.DMA((4,)),
        ],
        compiler_params=pltpu.CompilerParams(
            collective_id=0, has_side_effects=True, vmem_limit_bytes=48 << 20
        ),
    )(
        x_saved.reshape(2, 32, 256), gate_pre, up_pre, out_grad.reshape(2, 32, 256),
        gate_weight, up_weight, down_weight, gate_mask, up_mask, down_mask,
    )
    return (outs[0].reshape(64, 256), *outs[1:])


def solution(mesh):
    return jax.shard_map(
        on_device,
        mesh=mesh,
        in_specs=(
            P("dep", ("inp", "out")),
            P(("inp", "out"), "dep"),
            P(("inp", "out"), "dep"),
            P("dep", ("inp", "out")),
            P(("inp", "out"), "dep"),
            P(("inp", "out"), "dep"),
            P("dep", ("inp", "out")),
            P(("inp", "out"), "dep"),
            P(("inp", "out"), "dep"),
            P("dep", ("inp", "out")),
        ),
        out_specs=(
            P("dep", ("inp", "out")),
            P(("inp", "out"), "dep"),
            P(("inp", "out"), "dep"),
            P("dep", ("inp", "out")),
        ),
        check_vma=False,
    )
```

time: 518 us -> 122 us (0.24)
  the two profiles are of different devices: /device:TPU:24 before, /device:TPU:144 now
where the time goes in v1:
time: 122 us; the launch traced here: 121 us
  Pallas kernels  110 us (90%)
  local copies, waits for them, and re-layouts  11 us (9%)
    pallas_call x1, Pallas kernels, on_device(): pl.pallas_call(kernel, name='backward', out_shape=(jax.ShapeDtypeStruct((...  110 us
    unnamed x25, local copies, waits for them, and re-layouts  11 us

profile of v1, /device:TPU:144, one launch (start us, length us, event | category | flops | bytes accessed | tf_op | source)
XLA Modules:
  0.0 121.2 jit_solution(3210251530252686713)
XLA Ops:
  0.6 0.0 copy-start.9
  0.6 0.7 copy-done.9
  1.3 0.0 copy-start.7
  1.3 0.0 copy-start.8
  1.3 0.1 copy.14.dm
  1.4 0.6 copy-done.7
  2.0 0.0 copy-done.8
  2.0 0.0 copy-start
  2.0 1.0 copy-done
  3.0 0.0 copy-start.1
  3.0 1.0 copy-done.1
  4.0 0.0 copy-start.2
  4.0 1.0 copy-done.2
  5.1 0.0 copy-start.3
  5.1 0.8 copy-done.3
  5.9 0.0 copy-start.4
  5.9 0.8 copy-done.4
  6.7 0.0 copy-start.5
  6.7 0.8 copy-done.5
  7.5 0.0 copy-start.6
  7.5 0.8 copy-done.6
  8.2 109.6 %backward.1 = (bf16[2,32,256]{2,1,0:T(8,128)(2,1)S(1)}, f32[256,896]{1,0:T(8,128)S(1)}, f32[256,896]{1,0:T(8,128)S(1)}, f32[896,256]{1,0:T(8,128)S(1)}) custom-call(bf16[2,32,256]{2,1,0:T(8,128)(2,1)S(1)} %bitcast.3, bf16[32,896]{1,0:T(8,128)(2,1)S(1)} %copy-done.3, bf16[32,896]{1,0:T(8,128)(2,1)S(1)} %copy-done.4, bf16[2,32,256]{2,1,0:T(8,128)(2,1)S(1)} %bitcast.4, ...), custom_call_target="tpu_custom_call" | custom-call | tf_op jit(solution)/shard_map/backward/pallas_call | solution.py:358
  117.8 0.6 copy.19
  118.4 0.9 copy.20
  119.3 0.9 copy.21
  120.3 0.9 copy.22
Async XLA Ops:
  0.6 0.7 copy-start.9
  1.3 0.7 copy-start.7
  1.3 0.7 copy-start.8
  2.0 1.0 copy-start
  3.0 1.0 copy-start.1
  4.0 1.0 copy-start.2
  5.1 0.8 copy-start.3
  5.9 0.8 copy-start.4
  6.7 0.8 copy-start.5
  7.5 0.8 copy-start.6

commit v2 on v1

v2 whole, which is shorter than its diff:
```python
import functools

import jax
import jax.numpy as jnp
from jax import lax
from jax.experimental import pallas as pl
from jax.experimental.pallas import tpu as pltpu
from jax.sharding import PartitionSpec as P

TILE = 128
MESH = pl.DeviceIdType.MESH
F32 = jnp.float32
BF16 = jnp.bfloat16
NT = (((1,), (1,)), ((), ()))
TN = (((0,), (0,)), ((), ()))


def dot(left, right, dims):
    return lax.dot_general(left, right, dims, preferred_element_type=F32)


class Sems:
    def __init__(self, send, recv):
        self.send, self.recv = send, recv
        self.sends = self.recvs = 0
        self.started = []

    def take(self, count=1):
        first = self.recvs
        self.recvs += count
        return first

    def start(self, src, dst, slot, device):
        copy = pltpu.make_async_remote_copy(
            src_ref=src,
            dst_ref=dst,
            send_sem=self.send.at[self.sends],
            recv_sem=self.recv.at[slot],
            device_id=device,
            device_id_type=MESH,
        )
        self.sends += 1
        copy.start()
        self.started.append(copy)
        return copy

    def settle(self, copies):
        for copy in copies:
            copy.wait_send()
            self.started = [one for one in self.started if one is not copy]

    def wait(self, dst, slot, device):
        pltpu.make_async_remote_copy(
            src_ref=dst,
            dst_ref=dst,
            send_sem=self.send.at[0],
            recv_sem=self.recv.at[slot],
            device_id=device,
            device_id_type=MESH,
        ).wait_recv()

    def drain(self):
        for copy in self.started:
            copy.wait_send()


def keep_tiles(ref, mask, tiles=(2, 7), where=()):
    rows, cols = tiles
    for i in range(rows):
        for j in range(cols):
            at = (*where, pl.ds(i * TILE, TILE), pl.ds(j * TILE, TILE))
            ref[at] = (ref[at].astype(F32) * mask(i, j).astype(F32)).astype(ref.dtype)


def kernel(
    x_in, g_in, u_in, og_in, gw_in, uw_in, dw_in, gm_in, um_in, dm_in,
    ig_out, gwg_out, uwg_out, dwg_out,
    cot, cot_other, xs, pre, hid, f_gate, f_up, act, gate, up, gw, uw, dw,
    part_own, part_send, part_recv, sum_send, sum_recv,
    ig_own, ig_send, ig_recv, ig_mine, zl_send, zl_recv, ig_res,
    gwg, uwg, dwg, gm, um, dm, local, send, recv, zl_ss, zl_rs,
):
    y = lax.axis_index("inp")
    out = lax.axis_index("out")
    dep = lax.axis_index("dep")
    zh, c = out // 2, out % 2
    zl, x = dep // 4, dep % 4
    other = 1 - c
    plus = lambda v, k: (v + k) % 4
    at_core = {"out": zh * 2 + other}
    at_y = lambda k: {"inp": plus(y, k)}
    at_zh = lambda k: {"out": plus(zh, k) * 2 + c}
    at_x = lambda k: {"dep": zl * 4 + plus(x, k)}
    at_zl = lambda k, core: {"out": zh * 2 + core, "dep": plus(zl, k) * 4 + x}

    loads = []

    def load(src, dst):
        copy = pltpu.make_async_copy(src, dst, local.at[len(loads)])
        copy.start()
        loads.append(copy)
        return copy


    def wait_load(copy):
        copy.wait()

    ld_og = load(og_in.at[pl.ds(c, 1)], cot.at[c, zl, pl.ds(x, 1)])
    ld_g = load(g_in, pre.at[0, c, y, zh])
    ld_u = load(u_in, pre.at[1, c, y, zh])
    ld_dw = load(dw_in, dw.at[c])
    ld_masks = [load(dm_in, dm), load(gm_in, gm), load(um_in, um)]
    ld_x = load(x_in, xs.at[:, zl, x])
    ld_gw = load(gw_in, gw)
    ld_uw = load(uw_in, uw)

    peers = [at_core]
    for k in (1, 2, 3):
        peers += [at_y(k), at_zh(k), at_x(k), at_zl(k, 0), at_zl(k, 1)]
    barrier = pltpu.get_barrier_semaphore()
    for device in peers:
        pl.semaphore_signal(barrier, inc=1, device_id=device, device_id_type=MESH)
    pl.semaphore_wait(barrier, len(peers))

    sems = Sems(send, recv)

    og_slot = sems.take(8)
    sems.start(og_in.at[other], cot.at[c, zl, x], og_slot + c, at_core)
    for k in (2, 1, 3):
        for h in (0, 1):
            sems.start(og_in.at[h], cot.at[c, zl, x], og_slot + 2 * k + c, at_zl(k, h))

    pre_z = sems.take(4)
    pre_y = sems.take(16)
    pre_c = sems.take(4)

    def pre_to_y(kz):
        block = pre.at[:, c, y, plus(zh, -kz)]
        return [sems.start(block, block, pre_y + 4 * k + kz, at_y(k)) for k in (1, 3, 2)]

    wait_load(ld_g)
    wait_load(ld_u)
    pre_to_y(0)

    def pre_to_z(k):
        block = pre.at[:, c, y, zh]
        sems.start(block, block, pre_z + k, at_zh(k))


    wait_load(ld_dw)
    for copy in ld_masks:
        wait_load(copy)
    keep_tiles(dw, lambda i, j: dm[j, i], (7, 2), (c,))
    dw_slot = sems.take()
    sems.start(dw.at[c], dw.at[c], dw_slot, at_core)

    wait_load(ld_og)
    sems.wait(cot.at[other, zl, x], og_slot + other, at_core)
    for k in (1, 3, 2):
        for f in (0, 1):
            sems.wait(cot.at[f, plus(zl, -k), x], og_slot + 2 * k + f, at_core)
    og_x = sems.take(4)
    for k in (2, 1, 3):
        sems.start(cot.at[:, :, x], cot.at[:, :, x], og_x + k, at_x(k))
    pre_to_z(1)
    pre_to_z(3)

    x_zl = sems.take(4)
    x_x = sems.take(4)
    for k in (2, 1, 3):
        sems.start(x_in, xs.at[:, zl, x], x_zl + k, at_zl(k, c))

    wait_load(ld_gw)
    keep_tiles(gw, lambda i, j: gm[i, j])
    wait_load(ld_uw)
    keep_tiles(uw, lambda i, j: um[i, j])
    sems.wait(dw.at[other], dw_slot, at_core)
    for k in (1, 3, 2):
        sems.wait(cot.at[:, :, plus(x, -k)], og_x + k, at_core)

    def partial(group):
        rows = [cot[f, group].reshape(128, 256) for f in (0, 1)]
        return dot(rows[0], dw[0], NT) + dot(rows[1], dw[1], NT)

    for k in (2, 1, 3):
        part_send[k - 1] = partial(plus(y, k)).astype(BF16).reshape(4, 32, 896)
    part_y = sems.take(16)
    for kz in (2, 1, 3, 0):
        block = plus(zh, kz)
        for k in (2, 1, 3):
            sems.start(
                part_send.at[k - 1, block], part_recv.at[k - 1, kz], part_y + 4 * k + kz, at_y(k)
            )
    part_own[...] = partial(y).reshape(4, 32, 896)

    pre_to_z(2)

    def pre_on(k):
        sems.wait(pre.at[:, c, y, plus(zh, -k)], pre_z + k, at_core)
        return pre_to_y(k)

    cot_slot = sems.take()
    sems.start(cot.at[other], cot_other, cot_slot, at_core)

    sum_z = sems.take(4)
    total = None
    for kz in (2, 1, 3, 0):
        for k in (1, 3, 2):
            sems.wait(part_recv.at[k - 1, kz], part_y + 4 * k + kz, at_core)
        total = part_own[plus(zh, kz)]
        for k in (1, 2, 3):
            total = total + part_recv[k - 1, kz].astype(F32)
        if kz:
            sum_send[kz - 1] = total.astype(BF16)
            sems.start(sum_send.at[kz - 1], sum_recv.at[kz - 1], sum_z + kz, at_zh(kz))
    part_own[0] = total

    def pre_to_core(k):
        block = pre.at[:, c, plus(y, -k)]
        sems.start(block, block, pre_c + k, at_core)

    moving = pre_on(1)

    wait_load(ld_x)
    for k in (1, 3, 2):
        sems.wait(xs.at[:, plus(zl, -k), x], x_zl + k, at_core)
    for k in (2, 1, 3):
        sems.start(xs.at[:, :, x], xs.at[:, :, x], x_x + k, at_x(k))

    sems.settle(moving)
    moving = pre_on(3)

    def factors(k):
        group = plus(y, -k)
        sems.wait(pre.at[:, other, group], pre_c + k, at_core)

        def block(n, carry):
            h, b = n // 4, n % 4
            g = pre[0, h, group, b].astype(F32)
            u = pre[1, h, group, b].astype(F32)
            s = 1.0 / (1.0 + jnp.exp(-g))
            gs = g * s
            act[h, b] = (gs * u).astype(BF16)
            f_up[h, group, b] = gs
            f_gate[h, group, b] = u * s * (1.0 + g * (1.0 - s))
            return carry

        lax.fori_loop(0, 8, block, 0)
        mine = cot[c, group].reshape(128, 256)
        theirs = cot_other[group].reshape(128, 256)
        for i in range(7):
            at = pl.ds(i * TILE, TILE)
            tile = dot(act[c, :, :, at].reshape(128, TILE), mine, TN)
            tile = tile + dot(act[other, :, :, at].reshape(128, TILE), theirs, TN)
            if k:
                tile = tile + dwg[at, :]
            dwg[at, :] = tile

    total = part_own[0]
    for kz in (1, 3, 2):
        sems.wait(sum_recv.at[kz - 1], sum_z + kz, at_core)
        total = total + sum_recv[kz - 1].astype(F32)

    hid[c, y, zh] = total.astype(BF16)
    hid_z = sems.take(4)
    hid_y = sems.take(16)
    hid_c0 = sems.take(4)
    hid_c = sems.take(4)
    for k in (1, 3, 2):
        block = hid.at[c, y, zh]
        sems.start(block, block, hid_z + k, at_zh(k))

    def hid_on(kz):
        block = hid.at[c, y, plus(zh, -kz)]
        for k in (1, 3, 2):
            sems.start(block, block, hid_y + 4 * k + kz, at_y(k))
        sems.start(block, block, hid_c0 + kz, at_core)

    hid_on(0)
    sems.settle(moving)
    pre_on(2)
    pre_to_core(0)
    sems.wait(cot_other, cot_slot, at_core)
    factors(0)


    def pre_arrive(k):
        group = plus(y, -k)
        for kz in (0, 1, 3, 2):
            sems.wait(pre.at[:, c, group, plus(zh, -kz)], pre_y + 4 * k + kz, at_core)
        pre_to_core(k)

    for k in (1, 3):
        sems.wait(hid.at[c, y, plus(zh, -k)], hid_z + k, at_core)
        hid_on(k)
    pre_arrive(1)
    pre_arrive(3)
    factors(1)
    sems.wait(hid.at[c, y, plus(zh, -2)], hid_z + 2, at_core)
    hid_on(2)
    factors(3)
    pre_arrive(2)

    ig_x = sems.take(16)

    def hid_arrive(k):
        group = plus(y, -k)
        for kz in (0, 1, 3, 2):
            sems.wait(hid.at[c, group, plus(zh, -kz)], hid_y + 4 * k + kz, at_core)
        sems.start(hid.at[c, group], hid.at[c, group], hid_c + k, at_core)

    def input_rows(k):
        group = plus(y, -k)
        if k:
            sems.wait(hid.at[other, group], hid_c + k, at_core)
        else:
            for kz in range(4):
                sems.wait(hid.at[other, group, plus(zh, -kz)], hid_c0 + kz, at_core)
        rows = hid[:, group].astype(F32)
        gate[k] = (rows * f_gate[:, group]).astype(BF16).reshape(256, 896)
        up[k] = (rows * f_up[:, group]).astype(BF16).reshape(256, 896)
        rows = dot(gate[k], gw[...], NT) + dot(up[k], uw[...], NT)
        rows = rows.reshape(2, 4, 32, 256)
        ig_send[k] = rows.astype(BF16)
        for j in (2, 1, 3):
            sems.start(
                ig_send.at[k, :, plus(x, j)], ig_recv.at[k, j - 1], ig_x + 4 * k + j, at_x(j)
            )
        own = rows[:, 0]
        for j in (1, 2, 3):
            own = jnp.where(x == j, rows[:, j], own)
        ig_own[k] = own

    def weight_rows(k):
        left = xs[:, plus(y, -k)].reshape(256, 256)
        for total_ref, rows_ref in ((gwg, gate), (uwg, up)):
            product = dot(left, rows_ref[k], TN)
            if k:
                product = product + total_ref[...]
            total_ref[...] = product

    def reduce_x(k):
        group = plus(y, -k)
        for j in (1, 3, 2):
            sems.wait(ig_recv.at[k, j - 1], ig_x + 4 * k + j, at_core)
        value = ig_own[k]
        for j in (0, 1, 2):
            value = value + ig_recv[k, j].astype(F32)

        @pl.when(group == zl)
        def _():
            ig_mine[...] = value

        @pl.when(group != zl)
        def _():
            zl_send[k] = value
            to_zl(k).start()

    def to_zl(k):
        group = plus(y, -k)
        return pltpu.make_async_remote_copy(
            src_ref=zl_send.at[k],
            dst_ref=zl_recv.at[zl],
            send_sem=zl_ss.at[k],
            recv_sem=zl_rs.at[zl],
            device_id={"dep": group * 4 + x},
            device_id_type=MESH,
        )

    input_rows(0)
    for k in (1, 3, 2):
        sems.wait(xs.at[:, :, plus(x, -k)], x_x + k, at_core)
    weight_rows(0)
    factors(2)
    keep_tiles(dwg, lambda i, j: dm[j, i], (7, 2))
    stores = [load(dwg, dwg_out)]
    reduce_x(0)
    hid_arrive(1)
    hid_arrive(3)
    input_rows(1)
    input_rows(3)
    hid_arrive(2)
    weight_rows(1)
    input_rows(2)
    reduce_x(1)
    reduce_x(3)
    weight_rows(3)
    weight_rows(2)
    keep_tiles(gwg, lambda i, j: gm[i, j])
    stores.append(load(gwg, gwg_out))
    keep_tiles(uwg, lambda i, j: um[i, j])
    stores.append(load(uwg, uwg_out))
    reduce_x(2)

    value = ig_mine[...]
    for k in (1, 2, 3):
        source = plus(zl, k)
        pltpu.make_async_remote_copy(
            src_ref=zl_recv.at[source],
            dst_ref=zl_recv.at[source],
            send_sem=zl_ss.at[0],
            recv_sem=zl_rs.at[source],
            device_id=at_core,
            device_id_type=MESH,
        ).wait_recv()
        value = value + zl_recv[source]
    ig_res[...] = value.astype(BF16)
    stores.append(load(ig_res, ig_out))
    sems.drain()
    for k in range(4):

        @pl.when(plus(y, -k) != zl)
        def _():
            to_zl(k).wait_send()

    for copy in stores:
        copy.wait()


def store(*refs):
    copies = [
        pltpu.make_async_copy(src, dst, refs[8].at[n])
        for n, (src, dst) in enumerate(zip(refs[:4], refs[4:8]))
    ]
    for copy in copies:
        copy.start()
    for copy in copies:
        copy.wait()


SENDS = 128
RECVS = 128


def on_device(x_saved, gate_pre, up_pre, out_grad, gate_weight, up_weight, down_weight, gate_mask, up_mask, down_mask):
    any_ = pl.BlockSpec(memory_space=pl.ANY)
    hbm = pl.BlockSpec(memory_space=pltpu.HBM)
    vmem = lambda *shape: pltpu.VMEM(shape, BF16)
    vmem32 = lambda *shape: pltpu.VMEM(shape, F32)
    outs = pl.pallas_call(
        kernel,
        name="backward",
        out_shape=(
            jax.ShapeDtypeStruct((2, 32, 256), BF16),
            jax.ShapeDtypeStruct((256, 896), F32),
            jax.ShapeDtypeStruct((256, 896), F32),
            jax.ShapeDtypeStruct((896, 256), F32),
        ),
        in_specs=[hbm] * 10,
        out_specs=(any_,) * 4,
        scratch_shapes=[
            vmem(2, 4, 4, 32, 256),
            vmem(4, 4, 32, 256),
            vmem(2, 4, 4, 32, 256),
            vmem(2, 2, 4, 4, 32, 896),
            vmem(2, 4, 4, 32, 896),
            vmem32(2, 4, 4, 32, 896),
            vmem32(2, 4, 4, 32, 896),
            vmem(2, 4, 32, 896),
            vmem(4, 256, 896),
            vmem(4, 256, 896),
            vmem(256, 896),
            vmem(256, 896),
            vmem(2, 896, 256),
            vmem32(4, 32, 896),
            vmem(3, 4, 32, 896),
            vmem(3, 4, 32, 896),
            vmem(3, 32, 896),
            vmem(3, 32, 896),
            vmem32(4, 2, 32, 256),
            vmem(4, 2, 4, 32, 256),
            vmem(4, 3, 2, 32, 256),
            vmem32(2, 32, 256),
            vmem32(4, 2, 32, 256),
            vmem32(4, 2, 32, 256),
            vmem(2, 32, 256),
            vmem32(256, 896),
            vmem32(256, 896),
            vmem32(896, 256),
            pltpu.SMEM((2, 7), jnp.int32),
            pltpu.SMEM((2, 7), jnp.int32),
            pltpu.SMEM((2, 7), jnp.int32),
            pltpu.SemaphoreType.DMA((16,)),
            pltpu.SemaphoreType.DMA((SENDS,)),
            pltpu.SemaphoreType.DMA((RECVS,)),
            pltpu.SemaphoreType.DMA((4,)),
            pltpu.SemaphoreType.DMA((4,)),
        ],
        compiler_params=pltpu.CompilerParams(
            collective_id=0, has_side_effects=True, vmem_limit_bytes=48 << 20
        ),
    )(
        *(
            pltpu.with_memory_space_constraint(value, pltpu.HBM)
            for value in (
                x_saved.reshape(2, 32, 256), gate_pre, up_pre, out_grad.reshape(2, 32, 256),
                gate_weight, up_weight, down_weight, gate_mask, up_mask, down_mask.T,
            )
        ),
    )
    outs = pl.pallas_call(
        store,
        name="store",
        out_shape=[jax.ShapeDtypeStruct(value.shape, value.dtype) for value in outs],
        in_specs=[any_] * 4,
        out_specs=[hbm] * 4,
        scratch_shapes=[pltpu.SemaphoreType.DMA((4,))],
        compiler_params=pltpu.CompilerParams(vmem_limit_bytes=1 << 20),
    )(*(pltpu.with_memory_space_constraint(value, pltpu.VMEM) for value in outs))
    return (outs[0].reshape(64, 256), *outs[1:])


def solution(mesh):
    return jax.shard_map(
        on_device,
        mesh=mesh,
        in_specs=(
            P("dep", ("inp", "out")),
            P(("inp", "out"), "dep"),
            P(("inp", "out"), "dep"),
            P("dep", ("inp", "out")),
            P(("inp", "out"), "dep"),
            P(("inp", "out"), "dep"),
            P("dep", ("inp", "out")),
            P(("inp", "out"), "dep"),
            P(("inp", "out"), "dep"),
            P("dep", ("inp", "out")),
        ),
        out_specs=(
            P("dep", ("inp", "out")),
            P(("inp", "out"), "dep"),
            P(("inp", "out"), "dep"),
            P("dep", ("inp", "out")),
        ),
        check_vma=False,
    )
```

time: 122 us -> 95.7 us (0.78)
  the two profiles are of different devices: /device:TPU:144 before, /device:TPU:24 now
where the time goes in v2:
time: 95.7 us; the launch traced here: 94.4 us
  Pallas kernels  93.8 us (98%)
    pallas_call x1, Pallas kernels, on_device(): pl.pallas_call(kernel, name='backward', out_shape=(jax.ShapeDtypeStruct((...  92.2 us

profile of v2, /device:TPU:24, one launch (start us, length us, event | category | flops | bytes accessed | tf_op | source)
XLA Modules:
  0.0 94.4 jit_solution(17817321872192335685)
XLA Ops:
  0.6 92.2 %backward.1 = (bf16[2,32,256]{2,1,0:T(8,128)(2,1)S(1)}, f32[256,896]{1,0:T(8,128)S(1)}, f32[256,896]{1,0:T(8,128)S(1)}, f32[896,256]{1,0:T(8,128)S(1)}) custom-call(bf16[2,32,256]{2,1,0:T(8,128)(2,1)} %bitcast.4, bf16[32,896]{1,0:T(8,128)(2,1)} %g_in.1, bf16[32,896]{1,0:T(8,128)(2,1)} %u_in.1, bf16[2,32,256]{2,1,0:T(8,128)(2,1)} %bitcast.5, ...), custom_call_target="tpu_custom_call" | custom-call | tf_op jit(solution)/shard_map/backward/pallas_call | solution.py:440
  92.8 1.6 %store.1 = (bf16[2,32,256]{2,1,0:T(8,128)(2,1)}, f32[256,896]{1,0:T(8,128)}, f32[256,896]{1,0:T(8,128)}, f32[896,256]{1,0:T(8,128)}) custom-call(bf16[2,32,256]{2,1,0:T(8,128)(2,1)S(1)} %get-tuple-element.12.refs_0_, f32[256,896]{1,0:T(8,128)S(1)} %get-tuple-element.13.refs_1_, f32[256,896]{1,0:T(8,128)S(1)} %get-tuple-element.14.refs_2_, ...), custom_call_target="tpu_custom_call" | custom-call | tf_op jit(solution)/shard_map/store/pallas_call | solution.py:501

commit v3 on v2

--- a/solution.py
+++ b/solution.py
@@ -9,6 +9,7 @@
 
 TILE = 128
 MESH = pl.DeviceIdType.MESH
+PARTS = ((0, 512), (512, 384))
 F32 = jnp.float32
 BF16 = jnp.bfloat16
 NT = (((1,), (1,)), ((), ()))
@@ -44,11 +45,6 @@
         self.started.append(copy)
         return copy
 
-    def settle(self, copies):
-        for copy in copies:
-            copy.wait_send()
-            self.started = [one for one in self.started if one is not copy]
-
     def wait(self, dst, slot, device):
         pltpu.make_async_remote_copy(
             src_ref=dst,
@@ -74,11 +70,11 @@
 
 def kernel(
     x_in, g_in, u_in, og_in, gw_in, uw_in, dw_in, gm_in, um_in, dm_in,
-    ig_out, gwg_out, uwg_out, dwg_out,
+    ig_out, gwg, uwg, dwg,
     cot, cot_other, xs, pre, hid, f_gate, f_up, act, gate, up, gw, uw, dw,
-    part_own, part_send, part_recv, sum_send, sum_recv,
-    ig_own, ig_send, ig_recv, ig_mine, zl_send, zl_recv, ig_res,
-    gwg, uwg, dwg, gm, um, dm, local, send, recv, zl_ss, zl_rs,
+    part_own, part_send, part_recv, sum_mine, sum_send, sum_recv,
+    ig_all, ig_own, ig_send, ig_recv, ig_mine, zl_send, zl_recv,
+    gm, um, dm, local, send, recv, zh_ss, zh_rs, zl_ss, zl_rs,
 ):
     y = lax.axis_index("inp")
     out = lax.axis_index("out")
@@ -136,7 +132,8 @@
 
     def pre_to_y(kz):
         block = pre.at[:, c, y, plus(zh, -kz)]
-        return [sems.start(block, block, pre_y + 4 * k + kz, at_y(k)) for k in (1, 3, 2)]
+        for k in (1, 3):
+            sems.start(block, block, pre_y + 4 * k + kz, at_y(k))
 
     wait_load(ld_g)
     wait_load(ld_u)
@@ -145,6 +142,9 @@
     def pre_to_z(k):
         block = pre.at[:, c, y, zh]
         sems.start(block, block, pre_z + k, at_zh(k))
+
+    pre_to_z(1)
+    pre_to_z(3)
 
 
     wait_load(ld_dw)
@@ -154,81 +154,132 @@
     dw_slot = sems.take()
     sems.start(dw.at[c], dw.at[c], dw_slot, at_core)
 
+    og_x = sems.take(16)
+
+    def cot_to_x(kz):
+        block = cot.at[:, plus(zl, -kz), x]
+        for k in (1, 3, 2):
+            sems.start(block, block, og_x + 4 * k + kz, at_x(k))
+
     wait_load(ld_og)
     sems.wait(cot.at[other, zl, x], og_slot + other, at_core)
+    cot_to_x(0)
     for k in (1, 3, 2):
         for f in (0, 1):
             sems.wait(cot.at[f, plus(zl, -k), x], og_slot + 2 * k + f, at_core)
-    og_x = sems.take(4)
-    for k in (2, 1, 3):
-        sems.start(cot.at[:, :, x], cot.at[:, :, x], og_x + k, at_x(k))
-    pre_to_z(1)
-    pre_to_z(3)
+        cot_to_x(k)
 
     x_zl = sems.take(4)
     x_x = sems.take(4)
     for k in (2, 1, 3):
         sems.start(x_in, xs.at[:, zl, x], x_zl + k, at_zl(k, c))
 
+    sems.wait(dw.at[other], dw_slot, at_core)
+
+    units = [pl.ds(*part) for part in PARTS]
+    part_y = sems.take(32)
+
+    def partial(n, p):
+        column = plus(x, n)
+        if n and not p:
+            for kz in (0, 1, 3, 2):
+                sems.wait(
+                    cot.at[:, plus(zl, -kz), column], og_x + 4 * (4 - n) + kz, at_core
+                )
+        at = units[p]
+        rows = [cot[f, :, column].reshape(128, 256) for f in (0, 1)]
+        part = dot(rows[0], dw[0, at], NT) + dot(rows[1], dw[1, at], NT)
+        part = part.reshape(4, 32, PARTS[p][1])
+        part_own[n, :, :, at] = part
+        part_send[n, :, :, at] = part.astype(BF16)
+        for k in (2, 1, 3):
+            sems.start(
+                part_send.at[n, plus(y, k), :, at],
+                part_recv.at[n, k - 1, :, at],
+                part_y + 16 * p + 4 * n + k,
+                at_y(k),
+            )
+
+    for p in (0, 1):
+        for n in (0, 1, 3, 2):
+            partial(n, p)
+
     wait_load(ld_gw)
     keep_tiles(gw, lambda i, j: gm[i, j])
     wait_load(ld_uw)
     keep_tiles(uw, lambda i, j: um[i, j])
-    sems.wait(dw.at[other], dw_slot, at_core)
-    for k in (1, 3, 2):
-        sems.wait(cot.at[:, :, plus(x, -k)], og_x + k, at_core)
-
-    def partial(group):
-        rows = [cot[f, group].reshape(128, 256) for f in (0, 1)]
-        return dot(rows[0], dw[0], NT) + dot(rows[1], dw[1], NT)
-
-    for k in (2, 1, 3):
-        part_send[k - 1] = partial(plus(y, k)).astype(BF16).reshape(4, 32, 896)
-    part_y = sems.take(16)
-    for kz in (2, 1, 3, 0):
-        block = plus(zh, kz)
-        for k in (2, 1, 3):
-            sems.start(
-                part_send.at[k - 1, block], part_recv.at[k - 1, kz], part_y + 4 * k + kz, at_y(k)
-            )
-    part_own[...] = partial(y).reshape(4, 32, 896)
-
-    pre_to_z(2)
-
-    def pre_on(k):
-        sems.wait(pre.at[:, c, y, plus(zh, -k)], pre_z + k, at_core)
-        return pre_to_y(k)
 
     cot_slot = sems.take()
     sems.start(cot.at[other], cot_other, cot_slot, at_core)
 
-    sum_z = sems.take(4)
-    total = None
-    for kz in (2, 1, 3, 0):
+    def pre_opposite():
+        for k in (1, 3):
+            block = plus(zh, -k)
+            sems.wait(pre.at[:, c, y, block], pre_z + k, at_core)
+            block = pre.at[k // 2, c, y, block]
+            sems.start(block, block, pre_z + 2 - 2 * (k // 2), at_zh(k))
+
+    pre_opposite()
+
+    def to_zh(n, p):
+        return pltpu.make_async_remote_copy(
+            src_ref=sum_send.at[n, :, units[p]],
+            dst_ref=sum_recv.at[zh, :, units[p]],
+            send_sem=zh_ss.at[p, n],
+            recv_sem=zh_rs.at[p, zh],
+            device_id={"out": plus(x, n) * 2 + c},
+            device_id_type=MESH,
+        )
+
+    def sum_y(n, p):
+        at = units[p]
         for k in (1, 3, 2):
-            sems.wait(part_recv.at[k - 1, kz], part_y + 4 * k + kz, at_core)
-        total = part_own[plus(zh, kz)]
-        for k in (1, 2, 3):
-            total = total + part_recv[k - 1, kz].astype(F32)
-        if kz:
-            sum_send[kz - 1] = total.astype(BF16)
-            sems.start(sum_send.at[kz - 1], sum_recv.at[kz - 1], sum_z + kz, at_zh(kz))
-    part_own[0] = total
+            sems.wait(part_recv.at[n, k - 1, :, at], part_y + 16 * p + 4 * n + k, at_core)
+        total = part_own[n, y, :, at]
+        for k in (0, 1, 2):
+            total = total + part_recv[n, k, :, at].astype(F32)
+
+        @pl.when(plus(x, n) == zh)
+        def _():
+            sum_mine[:, at] = total
+
+        @pl.when(plus(x, n) != zh)
+        def _():
+            sum_send[n, :, at] = total.astype(BF16)
+            to_zh(n, p).start()
+
+    for n in (0, 1, 3, 2):
+        sum_y(n, 0)
+    for n in (0, 1, 3, 2):
+        sum_y(n, 1)
+
+    def zh_wait(p):
+        for k in (1, 3, 2):
+            source = plus(zh, k)
+            pltpu.make_async_remote_copy(
+                src_ref=sum_recv.at[source, :, units[p]],
+                dst_ref=sum_recv.at[source, :, units[p]],
+                send_sem=zh_ss.at[0, 0],
+                recv_sem=zh_rs.at[p, source],
+                device_id=at_core,
+                device_id_type=MESH,
+            ).wait_recv()
+
+    def zh_drain():
+        for p in (0, 1):
+            for n in range(4):
+
+                @pl.when(plus(x, n) != zh)
+                def _():
+                    to_zh(n, p).wait_send()
+
 
     def pre_to_core(k):
         block = pre.at[:, c, plus(y, -k)]
         sems.start(block, block, pre_c + k, at_core)
 
-    moving = pre_on(1)
-
-    wait_load(ld_x)
-    for k in (1, 3, 2):
-        sems.wait(xs.at[:, plus(zl, -k), x], x_zl + k, at_core)
-    for k in (2, 1, 3):
-        sems.start(xs.at[:, :, x], xs.at[:, :, x], x_x + k, at_x(k))
-
-    sems.settle(moving)
-    moving = pre_on(3)
+    pre_to_y(1)
+    pre_to_y(3)
 
     def factors(k):
         group = plus(y, -k)
@@ -256,71 +307,90 @@
                 tile = tile + dwg[at, :]
             dwg[at, :] = tile
 
-    total = part_own[0]
-    for kz in (1, 3, 2):
-        sems.wait(sum_recv.at[kz - 1], sum_z + kz, at_core)
-        total = total + sum_recv[kz - 1].astype(F32)
-
-    hid[c, y, zh] = total.astype(BF16)
-    hid_z = sems.take(4)
-    hid_y = sems.take(16)
-    hid_c0 = sems.take(4)
-    hid_c = sems.take(4)
+    hid_z = sems.take(8)
+    hid_y = sems.take(32)
+    hid_c0 = sems.take(8)
+    hid_c = sems.take(8)
+
+    def hid_on(kz, p):
+        block = hid.at[c, y, plus(zh, -kz), :, units[p]]
+        for k in (1, 3, 2):
+            sems.start(block, block, hid_y + 16 * p + 4 * k + kz, at_y(k))
+        sems.start(block, block, hid_c0 + 4 * p + kz, at_core)
+
+    def hid_begin(p):
+        at = units[p]
+        zh_wait(p)
+        total = sum_mine[:, at]
+        for k in (1, 2, 3):
+            total = total + sum_recv[plus(zh, k), :, at].astype(F32)
+        hid[c, y, zh, :, at] = total.astype(BF16)
+        block = hid.at[c, y, zh, :, at]
+        for k in (1, 3, 2):
+            sems.start(block, block, hid_z + 4 * p + k, at_zh(k))
+        hid_on(0, p)
+
+    def hid_next(k, p):
+        sems.wait(hid.at[c, y, plus(zh, -k), :, units[p]], hid_z + 4 * p + k, at_core)
+        hid_on(k, p)
+
+    hid_begin(0)
+    for n in (0, 1):
+        sems.wait(pre.at[n, c, y, plus(zh, -2)], pre_z + 2 - 2 * n, at_core)
+    pre_to_y(2)
+    hid_begin(1)
+    pre_to_core(0)
+
+    wait_load(ld_x)
     for k in (1, 3, 2):
-        block = hid.at[c, y, zh]
-        sems.start(block, block, hid_z + k, at_zh(k))
-
-    def hid_on(kz):
-        block = hid.at[c, y, plus(zh, -kz)]
-        for k in (1, 3, 2):
-            sems.start(block, block, hid_y + 4 * k + kz, at_y(k))
-        sems.start(block, block, hid_c0 + kz, at_core)
-
-    hid_on(0)
-    sems.settle(moving)
-    pre_on(2)
-    pre_to_core(0)
-    sems.wait(cot_other, cot_slot, at_core)
-    factors(0)
+        sems.wait(xs.at[:, plus(zl, -k), x], x_zl + k, at_core)
+    for k in (2, 1, 3):
+        sems.start(xs.at[:, :, x], xs.at[:, :, x], x_x + k, at_x(k))
 
 
     def pre_arrive(k):
         group = plus(y, -k)
+        if k == 2:
+            for n in (0, 1):
+                sems.wait(pre.at[n, c, group], pre_y + 8 + n, at_core)
+        else:
+            for kz in (0, 1, 3, 2):
+                sems.wait(pre.at[:, c, group, plus(zh, -kz)], pre_y + 4 * k + kz, at_core)
+            n = k // 2
+            block = pre.at[n, c, group]
+            sems.start(block, block, pre_y + 8 + n, at_y(k))
+        pre_to_core(k)
+
+
+    ig_x = sems.take(16)
+
+    def hid_arrive(k, p):
+        group, at = plus(y, -k), units[p]
         for kz in (0, 1, 3, 2):
-            sems.wait(pre.at[:, c, group, plus(zh, -kz)], pre_y + 4 * k + kz, at_core)
-        pre_to_core(k)
-
-    for k in (1, 3):
-        sems.wait(hid.at[c, y, plus(zh, -k)], hid_z + k, at_core)
-        hid_on(k)
-    pre_arrive(1)
-    pre_arrive(3)
-    factors(1)
-    sems.wait(hid.at[c, y, plus(zh, -2)], hid_z + 2, at_core)
-    hid_on(2)
-    factors(3)
-    pre_arrive(2)
-
-    ig_x = sems.take(16)
-
-    def hid_arrive(k):
-        group = plus(y, -k)
-        for kz in (0, 1, 3, 2):
-            sems.wait(hid.at[c, group, plus(zh, -kz)], hid_y + 4 * k + kz, at_core)
-        sems.start(hid.at[c, group], hid.at[c, group], hid_c + k, at_core)
-
-    def input_rows(k):
-        group = plus(y, -k)
+            sems.wait(
+                hid.at[c, group, plus(zh, -kz), :, at], hid_y + 16 * p + 4 * k + kz, at_core
+            )
+        block = hid.at[c, group, :, :, at]
+        sems.start(block, block, hid_c + 4 * p + k, at_core)
+
+    def input_rows(k, p):
+        group, at = plus(y, -k), units[p]
         if k:
-            sems.wait(hid.at[other, group], hid_c + k, at_core)
+            sems.wait(hid.at[other, group, :, :, at], hid_c + 4 * p + k, at_core)
         else:
             for kz in range(4):
-                sems.wait(hid.at[other, group, plus(zh, -kz)], hid_c0 + kz, at_core)
-        rows = hid[:, group].astype(F32)
-        gate[k] = (rows * f_gate[:, group]).astype(BF16).reshape(256, 896)
-        up[k] = (rows * f_up[:, group]).astype(BF16).reshape(256, 896)
-        rows = dot(gate[k], gw[...], NT) + dot(up[k], uw[...], NT)
+                sems.wait(
+                    hid.at[other, group, plus(zh, -kz), :, at], hid_c0 + 4 * p + kz, at_core
+                )
+        rows = hid[:, group, :, :, at].astype(F32)
+        gate[k, :, at] = (rows * f_gate[:, group, :, :, at]).astype(BF16).reshape(256, -1)
+        up[k, :, at] = (rows * f_up[:, group, :, :, at]).astype(BF16).reshape(256, -1)
+        rows = dot(gate[k, :, at], gw[:, at], NT) + dot(up[k, :, at], uw[:, at], NT)
         rows = rows.reshape(2, 4, 32, 256)
+        if not p:
+            ig_all[k] = rows
+            return
+        rows = rows + ig_all[k]
         ig_send[k] = rows.astype(BF16)
         for j in (2, 1, 3):
             sems.start(
@@ -331,13 +401,14 @@
             own = jnp.where(x == j, rows[:, j], own)
         ig_own[k] = own
 
-    def weight_rows(k):
+    def weight_rows(k, p):
+        at = units[p]
         left = xs[:, plus(y, -k)].reshape(256, 256)
         for total_ref, rows_ref in ((gwg, gate), (uwg, up)):
-            product = dot(left, rows_ref[k], TN)
+            product = dot(left, rows_ref[k, :, at], TN)
             if k:
-                product = product + total_ref[...]
-            total_ref[...] = product
+                product = product + total_ref[:, at]
+            total_ref[:, at] = product
 
     def reduce_x(k):
         group = plus(y, -k)
@@ -367,30 +438,50 @@
             device_id_type=MESH,
         )
 
-    input_rows(0)
+    sems.wait(cot_other, cot_slot, at_core)
+    factors(0)
+    for k in (1, 3, 2):
+        hid_next(k, 0)
+    pre_arrive(1)
+    pre_arrive(3)
+    input_rows(0, 0)
+    factors(1)
+    hid_next(1, 1)
+    hid_next(3, 1)
     for k in (1, 3, 2):
         sems.wait(xs.at[:, :, plus(x, -k)], x_x + k, at_core)
-    weight_rows(0)
+    weight_rows(0, 0)
+    hid_next(2, 1)
+    factors(3)
+    input_rows(0, 1)
+    hid_arrive(1, 0)
+    hid_arrive(3, 0)
+    weight_rows(0, 1)
+    input_rows(1, 0)
+    input_rows(3, 0)
+    pre_arrive(2)
+    hid_arrive(2, 0)
+    weight_rows(1, 0)
     factors(2)
+    weight_rows(3, 0)
+    input_rows(2, 0)
+    reduce_x(0)
+    weight_rows(2, 0)
+    hid_arrive(1, 1)
+    hid_arrive(3, 1)
+    hid_arrive(2, 1)
+    input_rows(1, 1)
+    input_rows(3, 1)
+    input_rows(2, 1)
+    weight_rows(1, 1)
+    reduce_x(1)
+    weight_rows(3, 1)
+    reduce_x(3)
+    weight_rows(2, 1)
+    reduce_x(2)
     keep_tiles(dwg, lambda i, j: dm[j, i], (7, 2))
-    stores = [load(dwg, dwg_out)]
-    reduce_x(0)
-    hid_arrive(1)
-    hid_arrive(3)
-    input_rows(1)
-    input_rows(3)
-    hid_arrive(2)
-    weight_rows(1)
-    input_rows(2)
-    reduce_x(1)
-    reduce_x(3)
-    weight_rows(3)
-    weight_rows(2)
     keep_tiles(gwg, lambda i, j: gm[i, j])
-    stores.append(load(gwg, gwg_out))
     keep_tiles(uwg, lambda i, j: um[i, j])
-    stores.append(load(uwg, uwg_out))
-    reduce_x(2)
 
     value = ig_mine[...]
     for k in (1, 2, 3):
@@ -404,17 +495,14 @@
             device_id_type=MESH,
         ).wait_recv()
         value = value + zl_recv[source]
-    ig_res[...] = value.astype(BF16)
-    stores.append(load(ig_res, ig_out))
+    ig_out[...] = value.astype(BF16)
     sems.drain()
+    zh_drain()
     for k in range(4):
 
         @pl.when(plus(y, -k) != zl)
         def _():
             to_zl(k).wait_send()
-
-    for copy in stores:
-        copy.wait()
 
 
 def store(*refs):
@@ -428,8 +516,8 @@
         copy.wait()
 
 
-SENDS = 128
-RECVS = 128
+SENDS = 160
+RECVS = 192
 
 
 def on_device(x_saved, gate_pre, up_pre, out_grad, gate_weight, up_weight, down_weight, gate_mask, up_mask, down_mask):
@@ -441,13 +529,13 @@
         kernel,
         name="backward",
         out_shape=(
-            jax.ShapeDtypeStruct((2, 32, 256), BF16),
-            jax.ShapeDtypeStruct((256, 896), F32),
-            jax.ShapeDtypeStruct((256, 896), F32),
-            jax.ShapeDtypeStruct((896, 256), F32),
+            vmem(2, 32, 256),
+            vmem32(256, 896),
+            vmem32(256, 896),
+            vmem32(896, 256),
         ),
         in_specs=[hbm] * 10,
-        out_specs=(any_,) * 4,
+        out_specs=(pl.BlockSpec(memory_space=pltpu.VMEM),) * 4,
         scratch_shapes=[
             vmem(2, 4, 4, 32, 256),
             vmem(4, 4, 32, 256),
@@ -462,27 +550,27 @@
             vmem(256, 896),
             vmem(256, 896),
             vmem(2, 896, 256),
-            vmem32(4, 32, 896),
-            vmem(3, 4, 32, 896),
-            vmem(3, 4, 32, 896),
-            vmem(3, 32, 896),
-            vmem(3, 32, 896),
+            vmem32(4, 4, 32, 896),
+            vmem(4, 4, 32, 896),
+            vmem(4, 3, 32, 896),
+            vmem32(32, 896),
+            vmem(4, 32, 896),
+            vmem(4, 32, 896),
+            vmem32(4, 2, 4, 32, 256),
             vmem32(4, 2, 32, 256),
             vmem(4, 2, 4, 32, 256),
             vmem(4, 3, 2, 32, 256),
             vmem32(2, 32, 256),
             vmem32(4, 2, 32, 256),
             vmem32(4, 2, 32, 256),
-            vmem(2, 32, 256),
-            vmem32(256, 896),
-            vmem32(256, 896),
-            vmem32(896, 256),
             pltpu.SMEM((2, 7), jnp.int32),
             pltpu.SMEM((2, 7), jnp.int32),
             pltpu.SMEM((2, 7), jnp.int32),
             pltpu.SemaphoreType.DMA((16,)),
             pltpu.SemaphoreType.DMA((SENDS,)),
             pltpu.SemaphoreType.DMA((RECVS,)),
+            pltpu.SemaphoreType.DMA((2, 4)),
+            pltpu.SemaphoreType.DMA((2, 4)),
             pltpu.SemaphoreType.DMA((4,)),
             pltpu.SemaphoreType.DMA((4,)),
         ],

time: 95.7 us -> 92 us (0.961); the launches traced: 94.4 us -> 91.8 us
  Pallas kernels: 93.8 us -> 91.2 us
    pallas_call x1, Pallas kernels: 92.2 us -> 89.6 us  [on_device(): pl.pallas_call(kernel, name='backward', out_shape=(vmem(2, 32, 256), vmem...]
where the time goes in v3:
time: 92 us; the launch traced here: 91.8 us
  Pallas kernels  91.2 us (99%)
    pallas_call x1, Pallas kernels, on_device(): pl.pallas_call(kernel, name='backward', out_shape=(vmem(2, 32, 256), vmem...  89.6 us

profile of v3, /device:TPU:24, one launch (start us, length us, event | category | flops | bytes accessed | tf_op | source)
XLA Modules:
  0.0 91.8 jit_solution(16156449939272022866)
XLA Ops:
  0.6 89.6 %backward.1 = (bf16[2,32,256]{2,1,0:T(8,128)(2,1)S(1)}, f32[256,896]{1,0:T(8,128)S(1)}, f32[256,896]{1,0:T(8,128)S(1)}, f32[896,256]{1,0:T(8,128)S(1)}) custom-call(bf16[2,32,256]{2,1,0:T(8,128)(2,1)} %bitcast.4, bf16[32,896]{1,0:T(8,128)(2,1)} %g_in.1, bf16[32,896]{1,0:T(8,128)(2,1)} %u_in.1, bf16[2,32,256]{2,1,0:T(8,128)(2,1)} %bitcast.5, ...), custom_call_target="tpu_custom_call" | custom-call | tf_op jit(solution)/shard_map/backward/pallas_call | solution.py:528
  90.3 1.6 %store.1 = (bf16[2,32,256]{2,1,0:T(8,128)(2,1)}, f32[256,896]{1,0:T(8,128)}, f32[256,896]{1,0:T(8,128)}, f32[896,256]{1,0:T(8,128)}) custom-call(bf16[2,32,256]{2,1,0:T(8,128)(2,1)S(1)} %get-tuple-element.12.refs_0_, f32[256,896]{1,0:T(8,128)S(1)} %get-tuple-element.13.refs_1_, f32[256,896]{1,0:T(8,128)S(1)} %get-tuple-element.14.refs_2_, ...), custom_call_target="tpu_custom_call" | custom-call | tf_op jit(solution)/shard_map/store/pallas_call | solution.py:589
